TPU v7x, 32 devices: a whole 2x2x4 slice. The times are simulated.
32 devices in a mesh: fsdp: 16 (over z, y, core), rep: 2 (over x), dp: 1.
Axes of the slice: x: 2, y: 2, z: 4, core: 2. Of those that a mesh axis runs over, the one named last changes fastest.
Arguments:
- trainer_gate: bfloat16 [8192, 1, 4096], P('fsdp', 'dp'), may hold values from -0.0625 to 0.0625
- trainer_up: bfloat16 [8192, 1, 4096], P('fsdp', 'dp'), may hold values from -0.0625 to 0.0625
- owner_map: int32 [64], replicated, may hold values from 0 to 63, each once
- sketch_seeds: int32 [8192], replicated, may hold values from 0 to 1
- probes: bfloat16 [2, 16, 128, 8192], P('rep', 'fsdp'), may hold values from -6 to 6
Outputs:
- digest: float32 [2, 64, 1, 4096], P(None, None, 'dp', 'fsdp')
- hidden: bfloat16 [2, 16, 128, 1, 256], P('rep', 'fsdp', None, 'dp')
Inputs may be any that keep to these rules, and one draw needn't show every extreme that they name: owner_map is a permutation: every true row block is held at exactly one trainer position.
All inputs are finite; a program needn't handle non-finite values.
Results may differ from a plain program's by a relative error of at most 0.01.
Values may be sent and summed in bfloat16 or wider, within the bound.
A program may use at most 64 MiB of HBM per device.

v0:
```python
import jax
import jax.numpy as jnp
from jax import lax
from jax.sharding import PartitionSpec as P


def on_device(trainer_gate, trainer_up, owner_map, sketch_seeds, probes):
    local_rows, local_dp, slice_width = trainer_gate.shape
    count_fsdp = lax.axis_size("fsdp")
    count_rep = lax.axis_size("rep")
    ranks = min(16, count_fsdp)
    subgroups = count_fsdp // ranks
    rank_width = slice_width // ranks
    narrow = rank_width // subgroups
    total_rows = local_rows * count_fsdp
    blocks_all = total_rows // 128
    local_blocks = local_rows // 128
    quarter = 128 // count_rep
    replica = lax.axis_index("rep")
    member = lax.axis_index("fsdp")
    subgroup = member % subgroups
    probe_rows = probes.shape[2]
    wide = probes.reshape(probe_rows, total_rows).astype(jnp.float32)
    meansq = jnp.mean(wide * wide, axis=-1, keepdims=True)
    normed = (wide / jnp.sqrt(meansq + 1e-05)).astype(jnp.bfloat16)

    def pick(matrix):
        viewed = matrix.reshape(local_blocks, count_rep, quarter, local_dp, ranks, 1, rank_width)
        chosen = lax.dynamic_slice_in_dim(viewed, replica, 1, 1)
        spread = jnp.broadcast_to(
            chosen, (local_blocks, 1, quarter, local_dp, ranks, subgroups, rank_width)
        )
        return spread.reshape(local_blocks * quarter, local_dp, count_fsdp * rank_width)

    gate_recv, up_recv = (
        lax.all_to_all(pick(trainer_gate), "fsdp", split_axis=2, concat_axis=0, tiled=True),
        lax.all_to_all(pick(trainer_up), "fsdp", split_axis=2, concat_axis=0, tiled=True),
    )
    positions = jnp.arange(blocks_all, dtype=jnp.int32)
    inverse = jnp.sum(
        jnp.where(owner_map[None, :] == positions[:, None], positions[None, :], 0), axis=1
    )

    def restore(matrix):
        return matrix.reshape(blocks_all, quarter, local_dp, rank_width)[inverse]

    gate_mine = restore(gate_recv)
    up_mine = restore(up_recv)
    all_signs = (1 - 2 * sketch_seeds).astype(jnp.float32).reshape(blocks_all, count_rep, quarter)

    def sketch(matrix, signs):
        part = lax.dynamic_slice_in_dim(matrix, subgroup * narrow, narrow, 3).astype(jnp.float32)
        return 8.0 * jnp.sum(signs[:, :, None, None] * part, axis=1)

    gate_full, up_full = (
        lax.all_gather(gate_mine, "rep", axis=1, tiled=True),
        lax.all_gather(up_mine, "rep", axis=1, tiled=True),
    )
    full_signs = all_signs.reshape(blocks_all, 128)
    digest = jnp.stack([sketch(gate_full, full_signs), sketch(up_full, full_signs)])
    gate_out = jnp.dot(
        normed,
        gate_full.reshape(total_rows, local_dp * rank_width),
        preferred_element_type=jnp.float32,
    )
    up_out = jnp.dot(
        normed,
        up_full.reshape(total_rows, local_dp * rank_width),
        preferred_element_type=jnp.float32,
    )
    hidden = (jax.nn.silu(gate_out) * up_out).astype(jnp.bfloat16)
    return (digest, hidden.reshape(1, 1, probe_rows, local_dp, rank_width))


def solution(mesh):
    placed = (P("fsdp", "dp", None), P("fsdp", "dp", None), P(), P(), P("rep", "fsdp", None, None))
    return jax.shard_map(
        on_device,
        mesh=mesh,
        in_specs=placed,
        out_specs=(P(None, None, "dp", "fsdp"), P("rep", "fsdp", None, "dp", None)),
        check_vma=False,
    )
```

profile of v0, /device:TPU:1, one launch (start us, length us, event | category | flops | bytes accessed | tf_op | source)
XLA Modules:
  0.0 300.1 jit_solution(3197805472370013089)
XLA Ops:
  7.2 5.8 %copy.39 = bf16[64,8,16,256]{3,2,1,0:T(8,128)(2,1)} copy(bf16[64,8,16,256]{3,1,2,0:T(8,128)(2,1)} %bitcast.72) | data formatting | bytes 8388608
  12.9 3.4 %copy.40 = bf16[64,8,16,256]{3,2,1,0:T(8,128)(2,1)} copy(bf16[64,8,16,256]{3,1,2,0:T(8,128)(2,1)S(1)} %bitcast.73) | data formatting | bytes 8388608
  16.3 4.5 %dynamic-slice_bitcast_fusion = (bf16[4,1,64,1,16,1,256]{6,4,2,0,5,3,1:T(8,128)(2,1)}, bf16[4,1,64,1,16,1,256]{6,4,2,0,5,3,1:T(8,128)(2,1)}) fusion(bf16[4,2,64,1,16,1,256]{6,4,2,1,0,5,3:T(8,128)(2,1)} %bitcast.67, s32[]{:T(128)S(6)} %select_n.26, bf16[4,2,64,1,16,1,256]{6,4,2,1,0,5,3:T(8,128)(2,1)} %bitcast.66), kind=kLoop, calls=%fused_computation.11 | loop fusion | bytes 8388612
  20.8 2.9 reshape.104
  23.6 7.3 %copy.29 = bf16[256,1,4096]{0,1,2:T(2,128)(2,1)} copy(bf16[256,1,4096]{2,0,1:T(8,128)(2,1)S(1)} %reshape.104) | data formatting | bytes 4194304 | tf_op jit(solution)/shard_map/reshape | solution.py:33
  30.9 0.5 broadcast.79
  31.5 21.6 %reduce.3 = bf16[4096,256]{1,0:T(8,128)(2,1)S(1)} reduce(bf16[4096,1,256]{2,1,0:T(2,128)(2,1)} %bitcast.60, bf16[]{:T(256)} %broadcast.79), dimensions={1}, to_apply=%bitcast.52.reduce_sub_computation | reduce | bytes 4194306
  53.0 2.1 reshape.140
  55.1 7.5 %all-to-all-start = ((bf16[16,2,32768]{2,1,0:T(2,128)(2,1)}), bf16[16,2,32768]{2,1,0:T(2,128)(2,1)S(1)}, u32[]{:S(2)}, u32[]{:S(2)}) async-start(bf16[16,2,32768]{2,1,0:T(2,128)(2,1)} %reshape.140), calls=%async_computation | async-start | bytes 4194304 | tf_op jit(solution)/shard_map/all_to_all | solution.py:36
  62.8 41.3 %all-to-all-done = bf16[16,2,32768]{2,1,0:T(2,128)(2,1)S(1)} async-done(((bf16[16,2,32768]{2,1,0:T(2,128)(2,1)}), bf16[16,2,32768]{2,1,0:T(2,128)(2,1)S(1)}, u32[]{:S(2)}, u32[]{:S(2)}) %all-to-all-start) | async-done | bytes 2097184 | tf_op jit(solution)/shard_map/all_to_all | solution.py:36
  104.1 6.8 %reshape.141 = bf16[4096,1,256]{2,1,0:T(2,128)(2,1)} reshape(bf16[16,2,32768]{2,1,0:T(2,128)(2,1)S(1)} %all-to-all-done) | data formatting | bytes 4194304
  110.8 2.5 copy.35
  113.4 2.4 copy.30
  115.8 3.6 %gather_fusion = bf16[64,64,256]{2,1,0:T(8,128)(2,1)} fusion(bf16[64,64,256]{2,1,0:T(8,128)(2,1)} %bitcast.71, s32[1024]{0:T(1024)S(1)} %pad_clamp_fusion), kind=kCustom, calls=%fused_computation | custom fusion | bytes 4194560 | tf_op jit(solution)/shard_map/gather | solution.py:45
  119.4 2.9 reshape.107
  122.3 7.4 %copy.32 = bf16[256,1,4096]{0,1,2:T(2,128)(2,1)} copy(bf16[256,1,4096]{2,0,1:T(8,128)(2,1)S(1)} %reshape.107) | data formatting | bytes 4194304 | tf_op jit(solution)/shard_map/reshape | solution.py:33
  129.7 21.7 %reduce.4 = bf16[4096,256]{1,0:T(8,128)(2,1)S(1)} reduce(bf16[4096,1,256]{2,1,0:T(2,128)(2,1)} %bitcast.61, bf16[]{:T(256)} %broadcast.79), dimensions={1}, to_apply=%bitcast.54.reduce_sub_computation | reduce | bytes 4194306
  151.3 2.1 reshape.142
  153.4 58.5 %all_to_all.30 = bf16[16,2,32768]{2,1,0:T(2,128)(2,1)S(1)} all-to-all(bf16[16,2,32768]{2,1,0:T(2,128)(2,1)} %reshape.142), channel_id=1, replica_groups=mesh['fsdp'=16,'rep'=2,'dp'=1] {'fsdp'}, dimensions={0} | all-to-all | bytes 4194304 | tf_op jit(solution)/shard_map/all_to_all | solution.py:37
  211.9 6.8 %reshape.143 = bf16[4096,1,256]{2,1,0:T(2,128)(2,1)} reshape(bf16[16,2,32768]{2,1,0:T(2,128)(2,1)S(1)} %all_to_all.30) | data formatting | bytes 4194304
  218.6 2.5 copy.36
  221.2 2.4 copy.33
  223.6 3.7 %gather_fusion.1 = bf16[64,64,256]{2,1,0:T(8,128)(2,1)} fusion(bf16[64,64,256]{2,1,0:T(8,128)(2,1)} %bitcast.70, s32[1024]{0:T(1024)S(1)} %pad_clamp_fusion), kind=kCustom, calls=%fused_computation.1 | custom fusion | bytes 4194560 | tf_op jit(solution)/shard_map/gather | solution.py:45
  227.2 1.6 copy-done.2
  228.8 0.5 fusion.2
  229.3 1.1 copy-done.3
  230.9 52.7 %all-gather.7.cloned.1.call-done = bf16[64,128,256]{2,1,0:T(8,128)(2,1)} async-done(((bf16[64,64,256]{2,1,0:T(8,128)(2,1)}), bf16[64,128,256]{2,1,0:T(8,128)(2,1)}) %all-gather.7.cloned.1.call-update) | async-done | bytes 4194320 | tf_op jit(solution)/shard_map/all_gather | solution.py:57
  283.6 5.1 %fusion.1 = (f32[64,256]{1,0:T(8,128)S(1)}, f32[64,256]{1,0:T(8,128)S(1)}) fusion(bf16[64,128,256]{2,1,0:T(8,128)(2,1)} %all-gather.5.cloned.1.call-done, f32[64,128]{1,0:T(8,128)S(1)} %convert_bitcast_fusion, bf16[64,128,256]{2,1,0:T(8,128)(2,1)} %all-gather.7.cloned.1.call-done), kind=kLoop, calls=%fused_computation.5 | loop fusion | flops 12550144 | bytes 8552448 | tf_op jit(solution)/shard_map/reduce_sum | solution.py:53
  288.9 0.8 pad_maximum_fusion
  289.7 0.8 fusion.8
  290.5 1.4 copy-done.1
  291.9 1.4 fusion.6
  (26 shorter events, 0.9 us)
Async XLA Ops:
  7.2 5.8 %copy-start.4 = (bf16[512,1,4096]{2,0,1:T(8,128)(2,1)S(1)}, bf16[512,1,4096]{2,0,1:T(8,128)(2,1)}, u32[]{:S(2)}) copy-start(bf16[512,1,4096]{2,0,1:T(8,128)(2,1)} %param.6) | copy-start | bytes 12582916
  55.1 7.5 %copy-start.6 = (s32[64]{0:T(128)S(1)}, s32[64]{0:T(128)}, u32[]{:S(2)}) copy-start(s32[64]{0:T(128)} %param.7) | copy-start | bytes 772
  55.1 48.9 %all-to-all-start = ((bf16[16,2,32768]{2,1,0:T(2,128)(2,1)}), bf16[16,2,32768]{2,1,0:T(2,128)(2,1)S(1)}, u32[]{:S(2)}, u32[]{:S(2)}) async-start(bf16[16,2,32768]{2,1,0:T(2,128)(2,1)} %reshape.140), calls=%async_computation | async-start | bytes 4194304 | tf_op jit(solution)/shard_map/all_to_all | solution.py:36
  62.6 168.3 %all-gather.5.cloned.1.call-start = ((), (), s32[]{:S(2)}) async-start(), calls=%async_computation.2 | async-start | bytes 6291456 | tf_op jit(solution)/shard_map/all_gather | solution.py:56
  119.4 164.3 %all-gather.7.cloned.1.call-start = ((), (), s32[]{:S(2)}) async-start(), calls=%async_computation.3 | async-start | bytes 6291456 | tf_op jit(solution)/shard_map/all_gather | solution.py:57
  227.2 1.6 copy-start.2
  227.2 2.1 copy-start.5
  228.8 1.6 copy-start.3
  283.6 6.1 %copy-start = (bf16[64,128,256]{2,1,0:T(8,128)(2,1)S(1)}, bf16[64,128,256]{2,1,0:T(8,128)(2,1)}, u32[]{:S(2)}) copy-start(bf16[64,128,256]{2,1,0:T(8,128)(2,1)} %all-gather.5.cloned.1.call-done) | copy-start | bytes 12582916
  289.7 2.2 copy-start.1
Sparse Core Ops, SparseCore 0:
  119.5 62.3 all-gather.4
  227.4 56.2 all-gather.6
where the time goes:
time: 301 us; the launch traced here: 300 us
  waiting for transfers between devices  94 us (31%)
  local copies, waits for them, and re-layouts  73.5 us (24%)
  blocking collectives  58.5 us (19%)
  other arithmetic  50.2 us (17%)
  between operations  14.2 us (5%)
  starting transfers between devices  7.56 us (3%)
    all_to_all x1, blocking collectives, on_device(): lax.all_to_all(pick(trainer_up), 'fsdp', split_axis=2, concat_axis=0, til...  58.5 us
    all_gather x1, waiting for transfers between devices, on_device(): lax.all_gather(up_mine, 'rep', axis=1, tiled=True)  52.7 us
    unnamed x2, other arithmetic  43.2 us
    all_to_all x1, waiting for transfers between devices, on_device(): lax.all_to_all(pick(trainer_gate), 'fsdp', split_axis=2, concat_axis=0, t...  41.3 us
    unnamed x24, local copies, waits for them, and re-layouts  40.9 us
    reshape x4, local copies, waits for them, and re-layouts, pick(): spread.reshape(local_blocks * quarter, local_dp, count_fsdp * rank_width)  20.4 us
    all_to_all x1, starting transfers between devices, on_device(): lax.all_to_all(pick(trainer_gate), 'fsdp', split_axis=2, concat_axis=0, t...  7.48 us
    gather x2, local copies, waits for them, and re-layouts, restore(): return matrix.reshape(blocks_all, quarter, local_dp, rank_width)[inverse]  7.23 us
  transfers between devices with their start and end apart: 3, of which 2 were waited for; matrix products, arithmetic and copies ran while one was open for 17% of the time, Pallas kernels for 0%

commit v1 on v0

v1 whole, which is shorter than its diff:
```python
import functools

import jax
import jax.numpy as jnp
from jax import lax
from jax.experimental import pallas as pl
from jax.experimental.pallas import tpu as pltpu
from jax.sharding import PartitionSpec as P

MESH = pl.DeviceIdType.MESH
LANES = 128


def kernel(
    count, group, subgroups, width, blocks,
    probes_hbm, gate_hbm, up_hbm, owner_hbm, seeds_hbm,
    digest_ref, hidden_ref,
    owner_ref, seeds_ref, x, gate, up, stage, got, part, part_in, total, plane_out, plane_in, dig_out, dig_in,
    x_load, load_sem, x_send, x_recv, p_send, p_recv, z_send, z_recv, d_send, d_recv,
):
    planes = count // group
    rows = x.shape[1]
    local_rows = gate.shape[0]
    nb = local_rows // LANES
    ranks = dig_out.shape[0]
    dig_rows = dig_out.shape[1]
    me = lax.axis_index("fsdp")
    plane, spot = me // group, me % group

    def peer(index):
        return {"fsdp": index}

    def remote(src, dst, send, recv, index):
        return pltpu.make_async_remote_copy(
            src_ref=src, dst_ref=dst, send_sem=send, recv_sem=recv,
            device_id=peer(index), device_id_type=MESH,
        )

    load_owner = pltpu.make_async_copy(owner_hbm, owner_ref, load_sem.at[2])
    load_seeds = pltpu.make_async_copy(seeds_hbm, seeds_ref, load_sem.at[3])
    load_owner.start()

    def load_x(block):
        columns = pl.ds(pl.multiple_of(block * LANES, LANES), LANES)
        return pltpu.make_async_copy(probes_hbm.at[:, columns], x.at[block], x_load.at[block])

    def start_x(block, carry):
        load_x(block).start()
        return carry

    def wait_x(block, carry):
        load_x(block).wait()
        return carry

    lax.fori_loop(0, blocks, start_x, 0)
    load_gate = pltpu.make_async_copy(gate_hbm, gate, load_sem.at[0])
    load_up = pltpu.make_async_copy(up_hbm, up, load_sem.at[1])
    load_gate.start()
    load_up.start()
    load_seeds.start()

    barrier = pltpu.get_barrier_semaphore()

    def greet(step, carry):
        pl.semaphore_signal(
            barrier, inc=1, device_id=peer((me + step) % count), device_id_type=MESH
        )
        return carry

    lax.fori_loop(1, count, greet, 0)
    load_owner.wait()
    lax.fori_loop(0, blocks, wait_x, 0)

    def pick(target, into):
        for i in range(nb):
            block = owner_ref[target * nb + i]
            into[target, :, i * LANES : (i + 1) * LANES] = x[block]

    phases = sorted(range(1, planes), key=lambda k: -min(k, planes - k))

    def x_copy(target):
        return remote(stage.at[target], got.at[me], x_send.at[target], x_recv.at[me], target)

    def x_arrival(source):
        return remote(stage.at[source], got.at[source], x_send.at[source], x_recv.at[source], source)

    pl.semaphore_wait(barrier, count - 1)
    def send(k, j):
        target = ((plane + k) % planes) * group + (spot + j) % group
        pick(target, stage)
        x_copy(target).start()

    def send_phase(k, last):
        def one(j, carry):
            send(k, j)
            return carry

        lax.fori_loop(1, last, one, 0)

    send_phase(phases[0], group + 1)
    send_phase(0, group)
    pick(me, got)

    def squares(block, acc):
        wide = x[block].astype(jnp.float32)
        return acc + wide * wide

    acc = lax.fori_loop(0, blocks, squares, jnp.zeros((rows, LANES), jnp.float32))
    meansq = jnp.sum(acc, axis=1, keepdims=True) / (blocks * LANES)
    scale = 1.0 / jnp.sqrt(meansq + 1e-05)

    load_seeds.wait()
    row_id = lax.broadcasted_iota(jnp.int32, (16, LANES), 0)
    for_gate, for_up = [], []
    for i in range(nb):
        held = lax.broadcasted_iota(jnp.int32, seeds_ref.shape, 0) == owner_ref[me * nb + i]
        seeds = jnp.sum(jnp.where(held, seeds_ref[...], 0), axis=0, keepdims=True)
        signs = jnp.broadcast_to(8 * (1 - 2 * seeds), (16, LANES)).astype(jnp.float32)
        for_gate.append(jnp.where(row_id == i, signs, 0.0))
        for_up.append(jnp.where(row_id == nb + i, signs, 0.0))
    for_gate = jnp.concatenate(for_gate, axis=1).astype(jnp.bfloat16)
    for_up = jnp.concatenate(for_up, axis=1).astype(jnp.bfloat16)
    load_gate.wait()
    load_up.wait()

    def columns_of(t):
        return pl.ds(pl.multiple_of(t * width, width), width)

    def sketch(t, carry):
        both = jnp.dot(for_gate, gate[:, columns_of(t)], preferred_element_type=jnp.float32)
        both += jnp.dot(for_up, up[:, columns_of(t)], preferred_element_type=jnp.float32)
        dig_out[t] = both[:dig_rows]
        return carry

    lax.fori_loop(0, ranks, sketch, 0)
    dig_in[me] = dig_out[me // subgroups]

    def d_copy(target):
        return remote(
            dig_out.at[target // subgroups], dig_in.at[me], d_send.at[target], d_recv.at[me], target
        )

    def d_arrival(source):
        return remote(
            dig_out.at[source // subgroups], dig_in.at[source], d_send.at[source],
            d_recv.at[source], source,
        )

    def send_digest(step, carry):
        d_copy((me + step) % count).start()
        return carry

    lax.fori_loop(1, count, send_digest, 0)

    def product(source):
        rows_of = got[source]
        columns = columns_of(source // subgroups)
        return (
            jnp.dot(rows_of, gate[:, columns], preferred_element_type=jnp.float32),
            jnp.dot(rows_of, up[:, columns], preferred_element_type=jnp.float32),
        )

    def p_copy(source_plane, spot_to):
        return remote(
            part.at[source_plane * group + spot_to],
            part_in.at[source_plane * group + spot],
            p_send.at[source_plane * group + spot_to],
            p_recv.at[source_plane * group + spot],
            plane * group + spot_to,
        )

    def p_arrival(source_plane, spot_from):
        index = source_plane * group + spot_from
        return remote(
            part.at[index], part_in.at[index], p_send.at[index], p_recv.at[index],
            plane * group + spot_from,
        )

    def z_copy(source_plane):
        return remote(
            plane_out.at[source_plane], plane_in.at[plane], z_send.at[source_plane],
            z_recv.at[plane], source_plane * group + spot,
        )

    def z_arrival(from_plane):
        return remote(
            plane_out.at[from_plane], plane_in.at[from_plane], z_send.at[from_plane],
            z_recv.at[from_plane], from_plane * group + spot,
        )

    def multiply(source_plane, k, following):
        def others(j, carry):
            spot_from = (spot + group - j) % group
            source = source_plane * group + spot_from
            x_arrival(source).wait_recv()
            if following is not None:
                send(following, j)
            a, b = product(source)
            part[source, :, :width] = a.astype(jnp.bfloat16)
            part[source, :, width:] = b.astype(jnp.bfloat16)
            p_copy(source_plane, spot_from).start()
            return carry

        lax.fori_loop(1, group, others, 0)
        source = source_plane * group + spot
        if k != 0:
            x_arrival(source).wait_recv()
            if following is not None:
                send(following, group)
        a, b = product(source)
        total[source_plane, :, :width] = a
        total[source_plane, :, width:] = b

    def reduce(source_plane):
        def add(j, carry):
            spot_from = (spot + group - j) % group
            p_arrival(source_plane, spot_from).wait_recv()
            total[source_plane] += part_in[source_plane * group + spot_from].astype(jnp.float32)
            return carry

        lax.fori_loop(1, group, add, 0)

    def reduce_away(source_plane):
        reduce(source_plane)
        plane_out[source_plane] = total[source_plane].astype(jnp.bfloat16)
        z_copy(source_plane).start()

    multiply(plane, 0, None)
    for p, k in enumerate(phases):
        source_plane = (plane + planes - k) % planes
        multiply(source_plane, k, phases[p + 1] if p + 1 < len(phases) else None)
        if p == 0:
            reduce(plane)
        else:
            reduce_away((plane + planes - phases[p - 1]) % planes)
    reduce_away((plane + planes - phases[-1]) % planes)

    def wait_digest(step, carry):
        d_arrival((me + step) % count).wait_recv()
        return carry

    lax.fori_loop(1, count, wait_digest, 0)
    span = count * dig_rows
    column = lax.broadcasted_iota(jnp.int32, (8, span), 1)
    inner = column % dig_rows
    place = jnp.where(inner < 2 * nb, (column // dig_rows) * nb + inner % nb, -1)
    owners = jnp.full((8, span), -1, jnp.int32)
    for j in range(blocks):
        owners = jnp.where(place == j, owner_ref[j], owners)
    owners = owners + jnp.where(inner >= nb, blocks, 0)
    owners = jnp.where(inner < 2 * nb, owners, -1)
    wanted = lax.broadcasted_iota(jnp.int32, (2 * blocks, span), 0)
    chosen = jnp.where(jnp.broadcast_to(owners[:1], (2 * blocks, span)) == wanted, 1.0, 0.0)
    digest_ref[...] = jnp.dot(
        chosen, dig_in[...].reshape(span, width),
        precision=lax.Precision.HIGHEST, preferred_element_type=jnp.float32,
    )

    def gather_planes(step, carry):
        from_plane = (plane + planes - step) % planes
        z_arrival(from_plane).wait_recv()
        total[plane] += plane_in[from_plane].astype(jnp.float32)
        return carry

    for k in phases:
        gather_planes(k, 0)
    gate_sum = total[plane, :, :width] * scale
    up_sum = total[plane, :, width:] * scale
    hidden_ref[...] = (gate_sum / (1.0 + jnp.exp(-gate_sum)) * up_sum).astype(jnp.bfloat16)

    def drain(step, carry):
        target = (me + step) % count
        x_copy(target).wait_send()
        d_copy(target).wait_send()
        return carry

    lax.fori_loop(1, count, drain, 0)

    def drain_plane(source_plane, carry):
        def drain_spot(j, inner_carry):
            p_copy(source_plane, (spot + group - j) % group).wait_send()
            return inner_carry

        return lax.fori_loop(1, group, drain_spot, carry)

    lax.fori_loop(0, planes, drain_plane, 0)

    def drain_away(step, carry):
        z_copy((plane + step) % planes).wait_send()
        return carry

    lax.fori_loop(1, planes, drain_away, 0)


def on_device(trainer_gate, trainer_up, owner_map, sketch_seeds, probes):
    local_rows, _, slice_width = trainer_gate.shape
    count = lax.axis_size("fsdp")
    ranks = min(16, count)
    subgroups = count // ranks
    width = slice_width // ranks
    narrow = width // subgroups
    group = 4
    planes = count // group
    total_rows = local_rows * count
    blocks = total_rows // LANES
    nb = local_rows // LANES
    dig_rows = -(-2 * nb // 8) * 8
    rows = probes.shape[2]
    bf16, f32 = jnp.bfloat16, jnp.float32
    dma = pltpu.SemaphoreType.DMA
    digest, hidden = pl.pallas_call(
        functools.partial(kernel, count, group, subgroups, width, blocks),
        out_shape=(
            jax.ShapeDtypeStruct((2 * blocks, width), f32),
            jax.ShapeDtypeStruct((rows, width), bf16),
        ),
        in_specs=[pl.BlockSpec(memory_space=pl.ANY)] * 5,
        out_specs=[pl.BlockSpec(memory_space=pltpu.VMEM)] * 2,
        scratch_shapes=[
            pltpu.SMEM((blocks,), jnp.int32),
            pltpu.VMEM((blocks, LANES), jnp.int32),
            pltpu.VMEM((blocks, rows, LANES), bf16),
            pltpu.VMEM((local_rows, slice_width), bf16),
            pltpu.VMEM((local_rows, slice_width), bf16),
            pltpu.VMEM((count, rows, local_rows), bf16),
            pltpu.VMEM((count, rows, local_rows), bf16),
            pltpu.VMEM((count, rows, 2 * width), bf16),
            pltpu.VMEM((count, rows, 2 * width), bf16),
            pltpu.VMEM((planes, rows, 2 * width), f32),
            pltpu.VMEM((planes, rows, 2 * width), bf16),
            pltpu.VMEM((planes, rows, 2 * width), bf16),
            pltpu.VMEM((ranks, dig_rows, width), f32),
            pltpu.VMEM((count, dig_rows, width), f32),
            dma((blocks,)), dma((4,)),
            dma((count,)), dma((count,)),
            dma((count,)), dma((count,)),
            dma((planes,)), dma((planes,)),
            dma((count,)), dma((count,)),
        ],
        compiler_params=pltpu.CompilerParams(
            collective_id=0, has_side_effects=True, vmem_limit_bytes=60 * 2**20
        ),
    )(
        probes.reshape(rows, total_rows),
        trainer_gate.reshape(local_rows, slice_width),
        trainer_up.reshape(local_rows, slice_width),
        owner_map,
        sketch_seeds.reshape(blocks, LANES),
    )
    if subgroups > 1:
        member = lax.axis_index("fsdp")
        digest = lax.dynamic_slice_in_dim(digest, (member % subgroups) * narrow, narrow, 1)
    return (
        digest.reshape(2, blocks, 1, narrow),
        hidden.reshape(1, 1, rows, 1, width),
    )


def solution(mesh):
    placed = (P("fsdp", "dp", None), P("fsdp", "dp", None), P(), P(), P("rep", "fsdp", None, None))
    return jax.shard_map(
        on_device,
        mesh=mesh,
        in_specs=placed,
        out_specs=(P(None, None, "dp", "fsdp"), P("rep", "fsdp", None, "dp", None)),
        check_vma=False,
    )
```

time: 301 us -> 75.5 us (0.25)
  the two profiles are of different devices: /device:TPU:1 before, /device:TPU:19 now
where the time goes in v1:
time: 75.5 us; the launch traced here: 75.3 us
  Pallas kernels  71.5 us (95%)
  local copies, waits for them, and re-layouts  3.17 us (4%)
    pallas_call x1, Pallas kernels, on_device(): pl.pallas_call(functools.partial(kernel, count, group, subgroups, width,...  71.5 us
    unnamed x2, local copies, waits for them, and re-layouts  3.17 us

profile of v1, /device:TPU:19, one launch (start us, length us, event | category | flops | bytes accessed | tf_op | source)
XLA Modules:
  0.0 75.3 jit_solution(11534031694901718559)
XLA Ops:
  0.6 71.5 %shard_map.68 = (f32[128,256]{1,0:T(8,128)}, bf16[128,256]{1,0:T(8,128)(2,1)}) custom-call(bf16[128,8192]{1,0:T(8,128)(2,1)} %bitcast.8, bf16[512,4096]{1,0:T(8,128)(2,1)} %bitcast.6, bf16[512,4096]{1,0:T(8,128)(2,1)} %bitcast.7, s32[64]{0:T(128)} %owner_hbm.1, s32[64,128]{1,0:T(8,128)} %bitcast.11), custom_call_target="tpu_custom_call" | custom-call | tf_op jit(solution)/shard_map/pallas_call | solution.py:311
  72.1 1.7 %copy.7 = f32[2,64,1,256]{3,2,1,0:T(1,128)} copy(f32[2,64,1,256]{3,1,0,2:T(8,128)} %bitcast.9) | data formatting | bytes 262144
  73.8 1.5 %copy.9 = bf16[1,1,128,1,256]{4,2,3,1,0:T(8,128)(2,1)} copy(bf16[1,1,128,1,256]{4,2,3,1,0:T(8,128)(2,1)} %bitcast.10) | data formatting | bytes 131072

commit v2 on v1

--- a/solution.py
+++ b/solution.py
@@ -76,7 +76,6 @@
             block = owner_ref[target * nb + i]
             into[target, :, i * LANES : (i + 1) * LANES] = x[block]
 
-    phases = sorted(range(1, planes), key=lambda k: -min(k, planes - k))
 
     def x_copy(target):
         return remote(stage.at[target], got.at[me], x_send.at[target], x_recv.at[me], target)
@@ -85,20 +84,28 @@
         return remote(stage.at[source], got.at[source], x_send.at[source], x_recv.at[source], source)
 
     pl.semaphore_wait(barrier, count - 1)
-    def send(k, j):
-        target = ((plane + k) % planes) * group + (spot + j) % group
+    def partner(m):
+        other = plane * 0
+        for bit in range((planes - 1).bit_length()):
+            digit = (plane // 2**bit) % 2
+            other = other + 2**bit * (1 - digit if (m >> bit) & 1 else digit)
+        return other
+
+    def send(m, j):
+        target = partner(m) * group + (spot + j) % group
         pick(target, stage)
         x_copy(target).start()
 
-    def send_phase(k, last):
+    def send_phase(m, last):
         def one(j, carry):
-            send(k, j)
+            send(m, j)
             return carry
 
         lax.fori_loop(1, last, one, 0)
 
-    send_phase(phases[0], group + 1)
+    send_phase(2, group + 1)
     send_phase(0, group)
+    send_phase(1, group + 1)
     pick(me, got)
 
     def squares(block, acc):
@@ -176,19 +183,15 @@
             plane * group + spot_from,
         )
 
-    def z_copy(source_plane):
-        return remote(
-            plane_out.at[source_plane], plane_in.at[plane], z_send.at[source_plane],
-            z_recv.at[plane], source_plane * group + spot,
-        )
-
-    def z_arrival(from_plane):
-        return remote(
-            plane_out.at[from_plane], plane_in.at[from_plane], z_send.at[from_plane],
-            z_recv.at[from_plane], from_plane * group + spot,
-        )
-
-    def multiply(source_plane, k, following):
+    def z_copy(m):
+        return remote(
+            plane_out.at[m], plane_in.at[m], z_send.at[m], z_recv.at[m],
+            partner(m if m % 2 else 1) * group + spot,
+        )
+
+    def multiply(m, following):
+        source_plane = partner(m)
+
         def others(j, carry):
             spot_from = (spot + group - j) % group
             source = source_plane * group + spot_from
@@ -203,37 +206,43 @@
 
         lax.fori_loop(1, group, others, 0)
         source = source_plane * group + spot
-        if k != 0:
+        if m != 0:
             x_arrival(source).wait_recv()
             if following is not None:
                 send(following, group)
         a, b = product(source)
-        total[source_plane, :, :width] = a
-        total[source_plane, :, width:] = b
-
-    def reduce(source_plane):
+        total[m, :, :width] = a
+        total[m, :, width:] = b
+
+    def reduce(m):
+        source_plane = partner(m)
+
         def add(j, carry):
             spot_from = (spot + group - j) % group
             p_arrival(source_plane, spot_from).wait_recv()
-            total[source_plane] += part_in[source_plane * group + spot_from].astype(jnp.float32)
+            total[m] += part_in[source_plane * group + spot_from].astype(jnp.float32)
             return carry
 
         lax.fori_loop(1, group, add, 0)
-
-    def reduce_away(source_plane):
-        reduce(source_plane)
-        plane_out[source_plane] = total[source_plane].astype(jnp.bfloat16)
-        z_copy(source_plane).start()
-
-    multiply(plane, 0, None)
-    for p, k in enumerate(phases):
-        source_plane = (plane + planes - k) % planes
-        multiply(source_plane, k, phases[p + 1] if p + 1 < len(phases) else None)
-        if p == 0:
-            reduce(plane)
-        else:
-            reduce_away((plane + planes - phases[p - 1]) % planes)
-    reduce_away((plane + planes - phases[-1]) % planes)
+        if m > 2 and m % 2:
+            add_plane(m, m - 1)
+        if m > 0:
+            plane_out[m] = total[m].astype(jnp.bfloat16)
+            z_copy(m).start()
+
+    def add_plane(m, arrived):
+        z_copy(arrived).wait_recv()
+        total[m] += plane_in[arrived].astype(jnp.float32)
+
+    steps = [0, 2, 1] + list(range(3, planes))
+    before = None
+    for m in steps:
+        following = m + 1 if m >= 2 and m + 1 < planes else None
+        multiply(m, following)
+        if before is not None:
+            reduce(before)
+        before = m
+    reduce(before)
 
     def wait_digest(step, carry):
         d_arrival((me + step) % count).wait_recv()
@@ -256,16 +265,10 @@
         precision=lax.Precision.HIGHEST, preferred_element_type=jnp.float32,
     )
 
-    def gather_planes(step, carry):
-        from_plane = (plane + planes - step) % planes
-        z_arrival(from_plane).wait_recv()
-        total[plane] += plane_in[from_plane].astype(jnp.float32)
-        return carry
-
-    for k in phases:
-        gather_planes(k, 0)
-    gate_sum = total[plane, :, :width] * scale
-    up_sum = total[plane, :, width:] * scale
+    for m in range(1, planes, 2):
+        add_plane(0, m)
+    gate_sum = total[0, :, :width] * scale
+    up_sum = total[0, :, width:] * scale
     hidden_ref[...] = (gate_sum / (1.0 + jnp.exp(-gate_sum)) * up_sum).astype(jnp.bfloat16)
 
     def drain(step, carry):
@@ -285,11 +288,8 @@
 
     lax.fori_loop(0, planes, drain_plane, 0)
 
-    def drain_away(step, carry):
-        z_copy((plane + step) % planes).wait_send()
-        return carry
-
-    lax.fori_loop(1, planes, drain_away, 0)
+    for m in range(1, planes):
+        z_copy(m).wait_send()
 
 
 def on_device(trainer_gate, trainer_up, owner_map, sketch_seeds, probes):

time: 75.5 us -> 70.2 us (0.930)
  the two profiles are of different devices: /device:TPU:19 before, /device:TPU:1 now
where the time goes in v2:
time: 70.2 us; the launch traced here: 69 us
  Pallas kernels  65.2 us (93%)
  local copies, waits for them, and re-layouts  3.17 us (5%)
    pallas_call x1, Pallas kernels, on_device(): pl.pallas_call(functools.partial(kernel, count, group, subgroups, width,...  65.2 us
    unnamed x2, local copies, waits for them, and re-layouts  3.17 us

profile of v2, /device:TPU:1, one launch (start us, length us, event | category | flops | bytes accessed | tf_op | source)
XLA Modules:
  0.0 69.0 jit_solution(6819887359229571590)
XLA Ops:
  0.6 65.2 %shard_map.68 = (f32[128,256]{1,0:T(8,128)}, bf16[128,256]{1,0:T(8,128)(2,1)}) custom-call(bf16[128,8192]{1,0:T(8,128)(2,1)} %bitcast.8, bf16[512,4096]{1,0:T(8,128)(2,1)} %bitcast.6, bf16[512,4096]{1,0:T(8,128)(2,1)} %bitcast.7, s32[64]{0:T(128)} %owner_hbm.1, s32[64,128]{1,0:T(8,128)} %bitcast.11), custom_call_target="tpu_custom_call" | custom-call | tf_op jit(solution)/shard_map/pallas_call | solution.py:311
  65.8 1.7 %copy.7 = f32[2,64,1,256]{3,2,1,0:T(1,128)} copy(f32[2,64,1,256]{3,1,0,2:T(8,128)} %bitcast.9) | data formatting | bytes 262144
  67.5 1.5 %copy.9 = bf16[1,1,128,1,256]{4,2,3,1,0:T(8,128)(2,1)} copy(bf16[1,1,128,1,256]{4,2,3,1,0:T(8,128)(2,1)} %bitcast.10) | data formatting | bytes 131072

commit v3 on v2

--- a/solution.py
+++ b/solution.py
@@ -189,60 +189,95 @@
             partner(m if m % 2 else 1) * group + spot,
         )
 
-    def multiply(m, following):
-        source_plane = partner(m)
-
+    def multiply_other(m, spot_from):
+        source = partner(m) * group + spot_from
+        a, b = product(source)
+        part[source, :, :width] = a.astype(jnp.bfloat16)
+        part[source, :, width:] = b.astype(jnp.bfloat16)
+        p_copy(partner(m), spot_from).start()
+
+    def multiply_own(m):
+        a, b = product(partner(m) * group + spot)
+        total[m, :, :width] = a
+        total[m, :, width:] = b
+
+    def start_following(m, j):
+        if m >= 2 and m + 1 < planes:
+            if m % 2:
+                send(m + 1, j)
+            else:
+                @pl.when((j - 1) // 2 == spot % 2)
+                def _():
+                    send(m + 1, 2 * ((j - 1) % 2) + 1)
+                    send(m + 1, 2 * ((j - 1) % 2) + 2)
+
+    def multiply(m):
         def others(j, carry):
             spot_from = (spot + group - j) % group
-            source = source_plane * group + spot_from
-            x_arrival(source).wait_recv()
-            if following is not None:
-                send(following, j)
-            a, b = product(source)
-            part[source, :, :width] = a.astype(jnp.bfloat16)
-            part[source, :, width:] = b.astype(jnp.bfloat16)
-            p_copy(source_plane, spot_from).start()
+            x_arrival(partner(m) * group + spot_from).wait_recv()
+            start_following(m, j)
+            multiply_other(m, spot_from)
             return carry
 
         lax.fori_loop(1, group, others, 0)
-        source = source_plane * group + spot
         if m != 0:
-            x_arrival(source).wait_recv()
-            if following is not None:
-                send(following, group)
-        a, b = product(source)
-        total[m, :, :width] = a
-        total[m, :, width:] = b
+            x_arrival(partner(m) * group + spot).wait_recv()
+            start_following(m, group)
+        multiply_own(m)
+
+    def multiply_staggered(m):
+        for half in range(2):
+            def one(step, carry, half=half):
+                j = 2 - (spot + half) % 2 + 2 * step
+                spot_from = (spot + group - j) % group
+                x_arrival(partner(m) * group + spot_from).wait_recv()
+                start_following(m, 2 * half + step + 1)
+
+                @pl.when(j == group)
+                def _():
+                    multiply_own(m)
+
+                @pl.when(j != group)
+                def _():
+                    multiply_other(m, spot_from)
+
+                return carry
+
+            lax.fori_loop(0, 2, one, 0)
+
+            @pl.when(spot % 2 == half)
+            def _():
+                reduce(m)
 
     def reduce(m):
-        source_plane = partner(m)
-
-        def add(j, carry):
+        summed = total[m]
+        for j in range(1, group):
             spot_from = (spot + group - j) % group
-            p_arrival(source_plane, spot_from).wait_recv()
-            total[m] += part_in[source_plane * group + spot_from].astype(jnp.float32)
-            return carry
-
-        lax.fori_loop(1, group, add, 0)
+            p_arrival(partner(m), spot_from).wait_recv()
         if m > 2 and m % 2:
-            add_plane(m, m - 1)
+            z_copy(m - 1).wait_recv()
+            summed += plane_in[m - 1].astype(jnp.float32)
+        for j in range(1, group):
+            spot_from = (spot + group - j) % group
+            summed += part_in[partner(m) * group + spot_from].astype(jnp.float32)
         if m > 0:
-            plane_out[m] = total[m].astype(jnp.bfloat16)
+            plane_out[m] = summed.astype(jnp.bfloat16)
             z_copy(m).start()
-
-    def add_plane(m, arrived):
-        z_copy(arrived).wait_recv()
-        total[m] += plane_in[arrived].astype(jnp.float32)
-
-    steps = [0, 2, 1] + list(range(3, planes))
-    before = None
-    for m in steps:
-        following = m + 1 if m >= 2 and m + 1 < planes else None
-        multiply(m, following)
-        if before is not None:
-            reduce(before)
-        before = m
-    reduce(before)
+        else:
+            total[m] = summed
+
+    multiply(0)
+    multiply(2)
+    reduce(0)
+    multiply(1)
+    reduce(2)
+    reduce(1)
+    for m in range(3, planes):
+        if m % 2:
+            multiply_staggered(m)
+        else:
+            multiply(m)
+            reduce(m)
 
     def wait_digest(step, carry):
         d_arrival((me + step) % count).wait_recv()
@@ -265,10 +300,12 @@
         precision=lax.Precision.HIGHEST, preferred_element_type=jnp.float32,
     )
 
+    summed = total[0]
     for m in range(1, planes, 2):
-        add_plane(0, m)
-    gate_sum = total[0, :, :width] * scale
-    up_sum = total[0, :, width:] * scale
+        z_copy(m).wait_recv()
+        summed += plane_in[m].astype(jnp.float32)
+    gate_sum = summed[:, :width] * scale
+    up_sum = summed[:, width:] * scale
     hidden_ref[...] = (gate_sum / (1.0 + jnp.exp(-gate_sum)) * up_sum).astype(jnp.bfloat16)
 
     def drain(step, carry):

time: 70.2 us -> 69.6 us (level)
  the two profiles are of different devices: /device:TPU:1 before, /device:TPU:11 now
where the time goes in v3:
time: 69.6 us; the launch traced here: 69.3 us
  Pallas kernels  65.5 us (94%)
  local copies, waits for them, and re-layouts  3.17 us (5%)
    pallas_call x1, Pallas kernels, on_device(): pl.pallas_call(functools.partial(kernel, count, group, subgroups, width,...  65.5 us
    unnamed x2, local copies, waits for them, and re-layouts  3.17 us

profile of v3, /device:TPU:11, one launch (start us, length us, event | category | flops | bytes accessed | tf_op | source)
XLA Modules:
  0.0 69.3 jit_solution(11735601245718312921)
XLA Ops:
  0.6 65.5 %shard_map.68 = (f32[128,256]{1,0:T(8,128)}, bf16[128,256]{1,0:T(8,128)(2,1)}) custom-call(bf16[128,8192]{1,0:T(8,128)(2,1)} %bitcast.8, bf16[512,4096]{1,0:T(8,128)(2,1)} %bitcast.6, bf16[512,4096]{1,0:T(8,128)(2,1)} %bitcast.7, s32[64]{0:T(128)} %owner_hbm.1, s32[64,128]{1,0:T(8,128)} %bitcast.11), custom_call_target="tpu_custom_call" | custom-call | tf_op jit(solution)/shard_map/pallas_call | solution.py:348
  66.2 1.7 %copy.7 = f32[2,64,1,256]{3,2,1,0:T(1,128)} copy(f32[2,64,1,256]{3,1,0,2:T(8,128)} %bitcast.9) | data formatting | bytes 262144
  67.9 1.5 %copy.9 = bf16[1,1,128,1,256]{4,2,3,1,0:T(8,128)(2,1)} copy(bf16[1,1,128,1,256]{4,2,3,1,0:T(8,128)(2,1)} %bitcast.10) | data formatting | bytes 131072

commit v4 on v3

--- a/solution.py
+++ b/solution.py
@@ -106,6 +106,11 @@
     send_phase(2, group + 1)
     send_phase(0, group)
     send_phase(1, group + 1)
+
+    @pl.when(spot % 2 == 0)
+    def _():
+        send_phase(3, group + 1)
+
     pick(me, got)
 
     def squares(block, acc):
@@ -206,7 +211,9 @@
             if m % 2:
                 send(m + 1, j)
             else:
-                @pl.when((j - 1) // 2 == spot % 2)
+                turn = (1 - spot % 2) * 2 if m == 2 else spot % 2
+
+                @pl.when((j - 1) // 2 == turn)
                 def _():
                     send(m + 1, 2 * ((j - 1) % 2) + 1)
                     send(m + 1, 2 * ((j - 1) % 2) + 2)
@@ -348,8 +355,8 @@
     digest, hidden = pl.pallas_call(
         functools.partial(kernel, count, group, subgroups, width, blocks),
         out_shape=(
-            jax.ShapeDtypeStruct((2 * blocks, width), f32),
-            jax.ShapeDtypeStruct((rows, width), bf16),
+            pltpu.VMEM((2 * blocks, width), f32),
+            pltpu.VMEM((rows, width), bf16),
         ),
         in_specs=[pl.BlockSpec(memory_space=pl.ANY)] * 5,
         out_specs=[pl.BlockSpec(memory_space=pltpu.VMEM)] * 2,

time: 69.6 us -> 65.6 us (0.943)
  the two profiles are of different devices: /device:TPU:11 before, /device:TPU:1 now
where the time goes in v4:
time: 65.6 us; the launch traced here: 65.5 us
  Pallas kernels  63.4 us (97%)
  local copies, waits for them, and re-layouts  1.42 us (2%)
    pallas_call x1, Pallas kernels, on_device(): pl.pallas_call(functools.partial(kernel, count, group, subgroups, width,...  63.4 us
    unnamed x2, local copies, waits for them, and re-layouts  1.42 us

profile of v4, /device:TPU:1, one launch (start us, length us, event | category | flops | bytes accessed | tf_op | source)
XLA Modules:
  0.0 65.5 jit_solution(9299227985057863780)
XLA Ops:
  0.6 63.4 %shard_map.68 = (f32[128,256]{1,0:T(8,128)S(1)}, bf16[128,256]{1,0:T(8,128)(2,1)S(1)}) custom-call(bf16[128,8192]{1,0:T(8,128)(2,1)} %bitcast.10, bf16[512,4096]{1,0:T(8,128)(2,1)} %bitcast.8, bf16[512,4096]{1,0:T(8,128)(2,1)} %bitcast.9, s32[64]{0:T(128)} %owner_hbm.1, s32[64,128]{1,0:T(8,128)} %bitcast.11), custom_call_target="tpu_custom_call" | custom-call | tf_op jit(solution)/shard_map/pallas_call | solution.py:355
  64.0 0.8 %copy.7 = f32[2,64,1,256]{3,2,1,0:T(1,128)} copy(f32[2,64,1,256]{3,1,0,2:T(8,128)S(1)} %bitcast.7) | data formatting | bytes 262144
  64.8 0.6 copy.9

commit v5 on v4

--- a/solution.py
+++ b/solution.py
@@ -15,7 +15,7 @@
     count, group, subgroups, width, blocks,
     probes_hbm, gate_hbm, up_hbm, owner_hbm, seeds_hbm,
     digest_ref, hidden_ref,
-    owner_ref, seeds_ref, x, gate, up, stage, got, part, part_in, total, plane_out, plane_in, dig_out, dig_in,
+    owner_ref, seeds_ref, x_flat, x, gate, up, stage, got, part, part_in, total, plane_out, plane_in, dig_out, dig_in,
     x_load, load_sem, x_send, x_recv, p_send, p_recv, z_send, z_recv, d_send, d_recv,
 ):
     planes = count // group
@@ -36,40 +36,37 @@
             device_id=peer(index), device_id_type=MESH,
         )
 
+    barrier = pltpu.get_barrier_semaphore()
+
+    def greet(step, carry):
+        pl.semaphore_signal(
+            barrier, inc=1, device_id=peer((me + step) % count), device_id_type=MESH
+        )
+        return carry
+
     load_owner = pltpu.make_async_copy(owner_hbm, owner_ref, load_sem.at[2])
     load_seeds = pltpu.make_async_copy(seeds_hbm, seeds_ref, load_sem.at[3])
-    load_owner.start()
-
-    def load_x(block):
-        columns = pl.ds(pl.multiple_of(block * LANES, LANES), LANES)
-        return pltpu.make_async_copy(probes_hbm.at[:, columns], x.at[block], x_load.at[block])
-
-    def start_x(block, carry):
-        load_x(block).start()
-        return carry
-
-    def wait_x(block, carry):
-        load_x(block).wait()
-        return carry
-
-    lax.fori_loop(0, blocks, start_x, 0)
     load_gate = pltpu.make_async_copy(gate_hbm, gate, load_sem.at[0])
     load_up = pltpu.make_async_copy(up_hbm, up, load_sem.at[1])
+    quarter = blocks // 4
+    loads = []
+    for c in range(4):
+        columns = pl.ds(c * quarter * LANES, quarter * LANES)
+        loads.append(
+            pltpu.make_async_copy(probes_hbm.at[:, columns], x_flat.at[:, columns], x_load.at[c])
+        )
+    load_owner.start()
+    for load in loads:
+        load.start()
+    lax.fori_loop(1, count, greet, 0)
     load_gate.start()
     load_up.start()
     load_seeds.start()
-
-    barrier = pltpu.get_barrier_semaphore()
-
-    def greet(step, carry):
-        pl.semaphore_signal(
-            barrier, inc=1, device_id=peer((me + step) % count), device_id_type=MESH
-        )
-        return carry
-
-    lax.fori_loop(1, count, greet, 0)
+    for c in range(4):
+        loads[c].wait()
+        for block in range(c * quarter, (c + 1) * quarter):
+            x[block] = x_flat[:, block * LANES : (block + 1) * LANES]
     load_owner.wait()
-    lax.fori_loop(0, blocks, wait_x, 0)
 
     def pick(target, into):
         for i in range(nb):
@@ -77,11 +74,28 @@
             into[target, :, i * LANES : (i + 1) * LANES] = x[block]
 
 
-    def x_copy(target):
-        return remote(stage.at[target], got.at[me], x_send.at[target], x_recv.at[me], target)
-
-    def x_arrival(source):
-        return remote(stage.at[source], got.at[source], x_send.at[source], x_recv.at[source], source)
+    half_rows = rows // 2
+
+    def rows_of(half):
+        return pl.ds(0, rows) if half is None else pl.ds(half * half_rows, half_rows)
+
+    def slot(index, half):
+        return index + count if half == 1 else index
+
+    def halves(m):
+        return (0, 1) if m > 2 and m % 2 else (None,)
+
+    def x_copy(target, half=None):
+        return remote(
+            stage.at[target, rows_of(half)], got.at[me, rows_of(half)],
+            x_send.at[slot(target, half)], x_recv.at[slot(me, half)], target,
+        )
+
+    def x_arrival(source, half=None):
+        return remote(
+            stage.at[source, rows_of(half)], got.at[source, rows_of(half)],
+            x_send.at[slot(source, half)], x_recv.at[slot(source, half)], source,
+        )
 
     pl.semaphore_wait(barrier, count - 1)
     def partner(m):
@@ -91,14 +105,17 @@
             other = other + 2**bit * (1 - digit if (m >> bit) & 1 else digit)
         return other
 
-    def send(m, j):
-        target = partner(m) * group + (spot + j) % group
-        pick(target, stage)
-        x_copy(target).start()
-
-    def send_phase(m, last):
+    def target_of(m, j):
+        return partner(m) * group + (spot + j) % group
+
+    def send(m, j, half=None):
+        if half != 1:
+            pick(target_of(m, j), stage)
+        x_copy(target_of(m, j), half).start()
+
+    def send_phase(m, last, half=None):
         def one(j, carry):
-            send(m, j)
+            send(m, j, half)
             return carry
 
         lax.fori_loop(1, last, one, 0)
@@ -109,7 +126,8 @@
 
     @pl.when(spot % 2 == 0)
     def _():
-        send_phase(3, group + 1)
+        send_phase(3, group + 1, 0)
+        send_phase(3, group + 1, 1)
 
     pick(me, got)
 
@@ -164,59 +182,64 @@
 
     lax.fori_loop(1, count, send_digest, 0)
 
-    def product(source):
-        rows_of = got[source]
+    def product(source, half=None):
+        rows_in = got[source, rows_of(half)]
         columns = columns_of(source // subgroups)
         return (
-            jnp.dot(rows_of, gate[:, columns], preferred_element_type=jnp.float32),
-            jnp.dot(rows_of, up[:, columns], preferred_element_type=jnp.float32),
-        )
-
-    def p_copy(source_plane, spot_to):
-        return remote(
-            part.at[source_plane * group + spot_to],
-            part_in.at[source_plane * group + spot],
-            p_send.at[source_plane * group + spot_to],
-            p_recv.at[source_plane * group + spot],
+            jnp.dot(rows_in, gate[:, columns], preferred_element_type=jnp.float32),
+            jnp.dot(rows_in, up[:, columns], preferred_element_type=jnp.float32),
+        )
+
+    def p_copy(source_plane, spot_to, half=None):
+        index, here = source_plane * group + spot_to, source_plane * group + spot
+        return remote(
+            part.at[index, rows_of(half)], part_in.at[here, rows_of(half)],
+            p_send.at[slot(index, half)], p_recv.at[slot(here, half)],
             plane * group + spot_to,
         )
 
-    def p_arrival(source_plane, spot_from):
+    def p_arrival(source_plane, spot_from, half=None):
         index = source_plane * group + spot_from
         return remote(
-            part.at[index], part_in.at[index], p_send.at[index], p_recv.at[index],
+            part.at[index, rows_of(half)], part_in.at[index, rows_of(half)],
+            p_send.at[slot(index, half)], p_recv.at[slot(index, half)],
             plane * group + spot_from,
         )
 
-    def z_copy(m):
-        return remote(
-            plane_out.at[m], plane_in.at[m], z_send.at[m], z_recv.at[m],
+    def z_copy(m, half=None):
+        index = m + planes if half == 1 else m
+        return remote(
+            plane_out.at[m, rows_of(half)], plane_in.at[m, rows_of(half)],
+            z_send.at[index], z_recv.at[index],
             partner(m if m % 2 else 1) * group + spot,
         )
 
-    def multiply_other(m, spot_from):
+    def multiply_other(m, spot_from, half=None):
         source = partner(m) * group + spot_from
-        a, b = product(source)
-        part[source, :, :width] = a.astype(jnp.bfloat16)
-        part[source, :, width:] = b.astype(jnp.bfloat16)
-        p_copy(partner(m), spot_from).start()
-
-    def multiply_own(m):
-        a, b = product(partner(m) * group + spot)
-        total[m, :, :width] = a
-        total[m, :, width:] = b
+        a, b = product(source, half)
+        part[source, rows_of(half), :width] = a.astype(jnp.bfloat16)
+        part[source, rows_of(half), width:] = b.astype(jnp.bfloat16)
+        p_copy(partner(m), spot_from, half).start()
+
+    def multiply_own(m, half=None):
+        a, b = product(partner(m) * group + spot, half)
+        total[m, rows_of(half), :width] = a
+        total[m, rows_of(half), width:] = b
 
     def start_following(m, j):
         if m >= 2 and m + 1 < planes:
             if m % 2:
                 send(m + 1, j)
-            else:
-                turn = (1 - spot % 2) * 2 if m == 2 else spot % 2
-
-                @pl.when((j - 1) // 2 == turn)
+                return
+            for half in halves(m + 1):
+                if m == 2:
+                    turn = (spot % 2) * (half + 1)
+                else:
+                    turn = 2 * (spot % 2) + half + 1
+
+                @pl.when(j == turn)
                 def _():
-                    send(m + 1, 2 * ((j - 1) % 2) + 1)
-                    send(m + 1, 2 * ((j - 1) % 2) + 2)
+                    send_phase(m + 1, group + 1, half)
 
     def multiply(m):
         def others(j, carry):
@@ -233,43 +256,45 @@
         multiply_own(m)
 
     def multiply_staggered(m):
-        for half in range(2):
-            def one(step, carry, half=half):
-                j = 2 - (spot + half) % 2 + 2 * step
-                spot_from = (spot + group - j) % group
-                x_arrival(partner(m) * group + spot_from).wait_recv()
-                start_following(m, 2 * half + step + 1)
-
-                @pl.when(j == group)
+        for odd in range(2):
+            for half in halves(m):
+                def one(step, carry, odd=odd, half=half):
+                    j = 2 - (spot + odd) % 2 + 2 * step
+                    spot_from = (spot + group - j) % group
+                    x_arrival(partner(m) * group + spot_from, half).wait_recv()
+                    if half == 1:
+                        start_following(m, 2 * odd + step + 1)
+
+                    @pl.when(j == group)
+                    def _():
+                        multiply_own(m, half)
+
+                    @pl.when(j != group)
+                    def _():
+                        multiply_other(m, spot_from, half)
+
+                    return carry
+
+                lax.fori_loop(0, 2, one, 0)
+
+                @pl.when(spot % 2 == odd)
                 def _():
-                    multiply_own(m)
-
-                @pl.when(j != group)
-                def _():
-                    multiply_other(m, spot_from)
-
-                return carry
-
-            lax.fori_loop(0, 2, one, 0)
-
-            @pl.when(spot % 2 == half)
-            def _():
-                reduce(m)
-
-    def reduce(m):
-        summed = total[m]
+                    reduce(m, half)
+
+    def reduce(m, half=None):
+        summed = total[m, rows_of(half)]
+        if m > 2 and m % 2:
+            if half == 0:
+                z_copy(m - 1).wait_recv()
+            summed += plane_in[m - 1, rows_of(half)].astype(jnp.float32)
         for j in range(1, group):
-            spot_from = (spot + group - j) % group
-            p_arrival(partner(m), spot_from).wait_recv()
-        if m > 2 and m % 2:
-            z_copy(m - 1).wait_recv()
-            summed += plane_in[m - 1].astype(jnp.float32)
+            p_arrival(partner(m), (spot + group - j) % group, half).wait_recv()
         for j in range(1, group):
-            spot_from = (spot + group - j) % group
-            summed += part_in[partner(m) * group + spot_from].astype(jnp.float32)
+            index = partner(m) * group + (spot + group - j) % group
+            summed += part_in[index, rows_of(half)].astype(jnp.float32)
         if m > 0:
-            plane_out[m] = summed.astype(jnp.bfloat16)
-            z_copy(m).start()
+            plane_out[m, rows_of(half)] = summed.astype(jnp.bfloat16)
+            z_copy(m, half).start()
         else:
             total[m] = summed
 
@@ -307,33 +332,40 @@
         precision=lax.Precision.HIGHEST, preferred_element_type=jnp.float32,
     )
 
-    summed = total[0]
-    for m in range(1, planes, 2):
-        z_copy(m).wait_recv()
-        summed += plane_in[m].astype(jnp.float32)
-    gate_sum = summed[:, :width] * scale
-    up_sum = summed[:, width:] * scale
-    hidden_ref[...] = (gate_sum / (1.0 + jnp.exp(-gate_sum)) * up_sum).astype(jnp.bfloat16)
-
-    def drain(step, carry):
-        target = (me + step) % count
-        x_copy(target).wait_send()
-        d_copy(target).wait_send()
+    def drain_digest(step, carry):
+        d_copy((me + step) % count).wait_send()
         return carry
 
-    lax.fori_loop(1, count, drain, 0)
-
-    def drain_plane(source_plane, carry):
-        def drain_spot(j, inner_carry):
-            p_copy(source_plane, (spot + group - j) % group).wait_send()
-            return inner_carry
-
-        return lax.fori_loop(1, group, drain_spot, carry)
-
-    lax.fori_loop(0, planes, drain_plane, 0)
+    lax.fori_loop(1, count, drain_digest, 0)
+    for m in range(planes):
+        for half in halves(m):
+            def drain_spot(j, carry, m=m, half=half):
+                x_copy(target_of(m, j), half).wait_send()
+                return carry
+
+            def drain_part(j, carry, m=m, half=half):
+                p_copy(partner(m), (spot + group - j) % group, half).wait_send()
+                return carry
+
+            lax.fori_loop(1, group + (m > 0), drain_spot, 0)
+            lax.fori_loop(1, group, drain_part, 0)
+
+    z_copy(1).wait_recv()
+    for half in range(2):
+        summed = total[0, rows_of(half)] + plane_in[1, rows_of(half)].astype(jnp.float32)
+        for m in range(3, planes, 2):
+            z_copy(m, half).wait_recv()
+            summed += plane_in[m, rows_of(half)].astype(jnp.float32)
+        factor = scale[half * half_rows : (half + 1) * half_rows]
+        gate_sum = summed[:, :width] * factor
+        up_sum = summed[:, width:] * factor
+        hidden_ref[rows_of(half)] = (
+            gate_sum / (1.0 + jnp.exp(-gate_sum)) * up_sum
+        ).astype(jnp.bfloat16)
 
     for m in range(1, planes):
-        z_copy(m).wait_send()
+        for half in halves(m):
+            z_copy(m, half).wait_send()
 
 
 def on_device(trainer_gate, trainer_up, owner_map, sketch_seeds, probes):
@@ -363,6 +395,7 @@
         scratch_shapes=[
             pltpu.SMEM((blocks,), jnp.int32),
             pltpu.VMEM((blocks, LANES), jnp.int32),
+            pltpu.VMEM((rows, total_rows), bf16),
             pltpu.VMEM((blocks, rows, LANES), bf16),
             pltpu.VMEM((local_rows, slice_width), bf16),
             pltpu.VMEM((local_rows, slice_width), bf16),
@@ -375,10 +408,10 @@
             pltpu.VMEM((planes, rows, 2 * width), bf16),
             pltpu.VMEM((ranks, dig_rows, width), f32),
             pltpu.VMEM((count, dig_rows, width), f32),
-            dma((blocks,)), dma((4,)),
-            dma((count,)), dma((count,)),
-            dma((count,)), dma((count,)),
-            dma((planes,)), dma((planes,)),
+            dma((4,)), dma((4,)),
+            dma((2 * count,)), dma((2 * count,)),
+            dma((2 * count,)), dma((2 * count,)),
+            dma((2 * planes,)), dma((2 * planes,)),
             dma((count,)), dma((count,)),
         ],
         compiler_params=pltpu.CompilerParams(

time: 65.6 us -> 67.6 us (1.030)
  Pallas kernels: 63.4 us -> 65.4 us
    pallas_call x1, Pallas kernels: 63.4 us -> 65.4 us  [on_device(): pl.pallas_call(functools.partial(kernel, count, group, subgroups, width,...]
where the time goes in v5:
time: 67.6 us; the launch traced here: 67.5 us
  Pallas kernels  65.4 us (97%)
  local copies, waits for them, and re-layouts  1.42 us (2%)
    pallas_call x1, Pallas kernels, on_device(): pl.pallas_call(functools.partial(kernel, count, group, subgroups, width,...  65.4 us
    unnamed x2, local copies, waits for them, and re-layouts  1.42 us

profile of v5, /device:TPU:1, one launch (start us, length us, event | category | flops | bytes accessed | tf_op | source)
XLA Modules:
  0.0 67.5 jit_solution(11109389045257220318)
XLA Ops:
  0.6 65.4 %shard_map.68 = (f32[128,256]{1,0:T(8,128)S(1)}, bf16[128,256]{1,0:T(8,128)(2,1)S(1)}) custom-call(bf16[128,8192]{1,0:T(8,128)(2,1)} %bitcast.10, bf16[512,4096]{1,0:T(8,128)(2,1)} %bitcast.8, bf16[512,4096]{1,0:T(8,128)(2,1)} %bitcast.9, s32[64]{0:T(128)} %owner_hbm.1, s32[64,128]{1,0:T(8,128)} %bitcast.11), custom_call_target="tpu_custom_call" | custom-call | tf_op jit(solution)/shard_map/pallas_call | solution.py:387
  66.1 0.8 %copy.7 = f32[2,64,1,256]{3,2,1,0:T(1,128)} copy(f32[2,64,1,256]{3,1,0,2:T(8,128)S(1)} %bitcast.7) | data formatting | bytes 262144
  66.9 0.6 copy.9

commit v6 on v5

--- a/solution.py
+++ b/solution.py
@@ -15,8 +15,8 @@
     count, group, subgroups, width, blocks,
     probes_hbm, gate_hbm, up_hbm, owner_hbm, seeds_hbm,
     digest_ref, hidden_ref,
-    owner_ref, seeds_ref, x_flat, x, gate, up, stage, got, part, part_in, total, plane_out, plane_in, dig_out, dig_in,
-    x_load, load_sem, x_send, x_recv, p_send, p_recv, z_send, z_recv, d_send, d_recv,
+    owner_ref, seeds_ref, x_flat, x, gate, up, stage, got, part, part_in, total, plane_out, plane_in, dig_out, dig_in, dig_mine, dig_theirs,
+    x_load, load_sem, x_send, x_recv, p_send, p_recv, z_send, z_recv, d_send, d_recv, e_sem,
 ):
     planes = count // group
     rows = x.shape[1]
@@ -26,6 +26,9 @@
     dig_rows = dig_out.shape[1]
     me = lax.axis_index("fsdp")
     plane, spot = me // group, me % group
+    replica = lax.axis_index("rep")
+    side = replica % 2
+    other_replica = {"rep": replica + 1 - 2 * side}
 
     def peer(index):
         return {"fsdp": index}
@@ -59,6 +62,7 @@
     for load in loads:
         load.start()
     lax.fori_loop(1, count, greet, 0)
+    pl.semaphore_signal(barrier, inc=1, device_id=other_replica, device_id_type=MESH)
     load_gate.start()
     load_up.start()
     load_seeds.start()
@@ -74,16 +78,14 @@
             into[target, :, i * LANES : (i + 1) * LANES] = x[block]
 
 
-    half_rows = rows // 2
-
     def rows_of(half):
-        return pl.ds(0, rows) if half is None else pl.ds(half * half_rows, half_rows)
+        return pl.ds(0, rows)
 
     def slot(index, half):
-        return index + count if half == 1 else index
+        return index
 
     def halves(m):
-        return (0, 1) if m > 2 and m % 2 else (None,)
+        return (None,)
 
     def x_copy(target, half=None):
         return remote(
@@ -97,7 +99,7 @@
             x_send.at[slot(source, half)], x_recv.at[slot(source, half)], source,
         )
 
-    pl.semaphore_wait(barrier, count - 1)
+    pl.semaphore_wait(barrier, count)
     def partner(m):
         other = plane * 0
         for bit in range((planes - 1).bit_length()):
@@ -126,8 +128,7 @@
 
     @pl.when(spot % 2 == 0)
     def _():
-        send_phase(3, group + 1, 0)
-        send_phase(3, group + 1, 1)
+        send_phase(3, group + 1)
 
     pick(me, got)
 
@@ -141,28 +142,42 @@
 
     load_seeds.wait()
     row_id = lax.broadcasted_iota(jnp.int32, (16, LANES), 0)
-    for_gate, for_up = [], []
+    for_left, for_right = [], []
     for i in range(nb):
         held = lax.broadcasted_iota(jnp.int32, seeds_ref.shape, 0) == owner_ref[me * nb + i]
         seeds = jnp.sum(jnp.where(held, seeds_ref[...], 0), axis=0, keepdims=True)
         signs = jnp.broadcast_to(8 * (1 - 2 * seeds), (16, LANES)).astype(jnp.float32)
-        for_gate.append(jnp.where(row_id == i, signs, 0.0))
-        for_up.append(jnp.where(row_id == nb + i, signs, 0.0))
-    for_gate = jnp.concatenate(for_gate, axis=1).astype(jnp.bfloat16)
-    for_up = jnp.concatenate(for_up, axis=1).astype(jnp.bfloat16)
+        for_left.append(jnp.where(row_id == i, signs, 0.0))
+        for_right.append(jnp.where(row_id == nb + i, signs, 0.0))
+    for_left = jnp.concatenate(for_left, axis=1).astype(jnp.bfloat16)
+    for_right = jnp.concatenate(for_right, axis=1).astype(jnp.bfloat16)
     load_gate.wait()
     load_up.wait()
 
     def columns_of(t):
         return pl.ds(pl.multiple_of(t * width, width), width)
 
-    def sketch(t, carry):
-        both = jnp.dot(for_gate, gate[:, columns_of(t)], preferred_element_type=jnp.float32)
-        both += jnp.dot(for_up, up[:, columns_of(t)], preferred_element_type=jnp.float32)
-        dig_out[t] = both[:dig_rows]
-        return carry
-
-    lax.fori_loop(0, ranks, sketch, 0)
+    half_width = width // 2
+
+    def sketch_all(weights):
+        def sketch(t, carry):
+            left = pl.ds(pl.multiple_of(t * width, width), half_width)
+            right = pl.ds(pl.multiple_of(t * width + half_width, half_width), half_width)
+            both = jnp.dot(for_left, weights[:, left], preferred_element_type=jnp.float32)
+            both += jnp.dot(for_right, weights[:, right], preferred_element_type=jnp.float32)
+            dig_out[t] = both[:dig_rows]
+            return carry
+
+        lax.fori_loop(0, ranks, sketch, 0)
+
+    @pl.when(side == 0)
+    def _():
+        sketch_all(gate)
+
+    @pl.when(side == 1)
+    def _():
+        sketch_all(up)
+
     dig_in[me] = dig_out[me // subgroups]
 
     def d_copy(target):
@@ -231,15 +246,12 @@
             if m % 2:
                 send(m + 1, j)
                 return
-            for half in halves(m + 1):
-                if m == 2:
-                    turn = (spot % 2) * (half + 1)
-                else:
-                    turn = 2 * (spot % 2) + half + 1
-
-                @pl.when(j == turn)
-                def _():
-                    send_phase(m + 1, group + 1, half)
+            turn = (1 - spot % 2) * 2 if m == 2 else spot % 2
+
+            @pl.when((j - 1) // 2 == turn)
+            def _():
+                send(m + 1, 2 * ((j - 1) % 2) + 1)
+                send(m + 1, 2 * ((j - 1) % 2) + 2)
 
     def multiply(m):
         def others(j, carry):
@@ -262,8 +274,7 @@
                     j = 2 - (spot + odd) % 2 + 2 * step
                     spot_from = (spot + group - j) % group
                     x_arrival(partner(m) * group + spot_from, half).wait_recv()
-                    if half == 1:
-                        start_following(m, 2 * odd + step + 1)
+                    start_following(m, 2 * odd + step + 1)
 
                     @pl.when(j == group)
                     def _():
@@ -284,8 +295,7 @@
     def reduce(m, half=None):
         summed = total[m, rows_of(half)]
         if m > 2 and m % 2:
-            if half == 0:
-                z_copy(m - 1).wait_recv()
+            z_copy(m - 1).wait_recv()
             summed += plane_in[m - 1, rows_of(half)].astype(jnp.float32)
         for j in range(1, group):
             p_arrival(partner(m), (spot + group - j) % group, half).wait_recv()
@@ -304,13 +314,6 @@
     multiply(1)
     reduce(2)
     reduce(1)
-    for m in range(3, planes):
-        if m % 2:
-            multiply_staggered(m)
-        else:
-            multiply(m)
-            reduce(m)
-
     def wait_digest(step, carry):
         d_arrival((me + step) % count).wait_recv()
         return carry
@@ -327,10 +330,28 @@
     owners = jnp.where(inner < 2 * nb, owners, -1)
     wanted = lax.broadcasted_iota(jnp.int32, (2 * blocks, span), 0)
     chosen = jnp.where(jnp.broadcast_to(owners[:1], (2 * blocks, span)) == wanted, 1.0, 0.0)
-    digest_ref[...] = jnp.dot(
-        chosen, dig_in[...].reshape(span, width),
+    ordered = jnp.dot(
+        chosen, dig_in[...].reshape(span, half_width),
         precision=lax.Precision.HIGHEST, preferred_element_type=jnp.float32,
     )
+    dig_mine[:, :half_width] = ordered[:blocks]
+    dig_mine[:, half_width:] = ordered[blocks:]
+    exchange = pltpu.make_async_remote_copy(
+        src_ref=dig_mine, dst_ref=dig_theirs, send_sem=e_sem.at[0], recv_sem=e_sem.at[1],
+        device_id=other_replica, device_id_type=MESH,
+    )
+    exchange.start()
+
+    for m in range(3, planes):
+        if m % 2:
+            multiply_staggered(m)
+        else:
+            multiply(m)
+            reduce(m)
+
+    digest_ref[pl.ds(pl.multiple_of(side * blocks, blocks), blocks), :] = dig_mine[...]
+    exchange.wait()
+    digest_ref[pl.ds(pl.multiple_of((1 - side) * blocks, blocks), blocks), :] = dig_theirs[...]
 
     def drain_digest(step, carry):
         d_copy((me + step) % count).wait_send()
@@ -350,18 +371,13 @@
             lax.fori_loop(1, group + (m > 0), drain_spot, 0)
             lax.fori_loop(1, group, drain_part, 0)
 
-    z_copy(1).wait_recv()
-    for half in range(2):
-        summed = total[0, rows_of(half)] + plane_in[1, rows_of(half)].astype(jnp.float32)
-        for m in range(3, planes, 2):
-            z_copy(m, half).wait_recv()
-            summed += plane_in[m, rows_of(half)].astype(jnp.float32)
-        factor = scale[half * half_rows : (half + 1) * half_rows]
-        gate_sum = summed[:, :width] * factor
-        up_sum = summed[:, width:] * factor
-        hidden_ref[rows_of(half)] = (
-            gate_sum / (1.0 + jnp.exp(-gate_sum)) * up_sum
-        ).astype(jnp.bfloat16)
+    summed = total[0]
+    for m in range(1, planes, 2):
+        z_copy(m).wait_recv()
+        summed += plane_in[m].astype(jnp.float32)
+    gate_sum = summed[:, :width] * scale
+    up_sum = summed[:, width:] * scale
+    hidden_ref[...] = (gate_sum / (1.0 + jnp.exp(-gate_sum)) * up_sum).astype(jnp.bfloat16)
 
     for m in range(1, planes):
         for half in halves(m):
@@ -406,13 +422,16 @@
             pltpu.VMEM((planes, rows, 2 * width), f32),
             pltpu.VMEM((planes, rows, 2 * width), bf16),
             pltpu.VMEM((planes, rows, 2 * width), bf16),
-            pltpu.VMEM((ranks, dig_rows, width), f32),
-            pltpu.VMEM((count, dig_rows, width), f32),
+            pltpu.VMEM((ranks, dig_rows, width // 2), f32),
+            pltpu.VMEM((count, dig_rows, width // 2), f32),
+            pltpu.VMEM((blocks, width), f32),
+            pltpu.VMEM((blocks, width), f32),
             dma((4,)), dma((4,)),
             dma((2 * count,)), dma((2 * count,)),
             dma((2 * count,)), dma((2 * count,)),
             dma((2 * planes,)), dma((2 * planes,)),
             dma((count,)), dma((count,)),
+            dma((2,)),
         ],
         compiler_params=pltpu.CompilerParams(
             collective_id=0, has_side_effects=True, vmem_limit_bytes=60 * 2**20

time: 67.6 us -> 72.3 us (1.070)
  Pallas kernels: 65.4 us -> 70.1 us
    pallas_call x1, Pallas kernels: 65.4 us -> 70.1 us  [on_device(): pl.pallas_call(functools.partial(kernel, count, group, subgroups, width,...]
where the time goes in v6:
time: 72.3 us; the launch traced here: 72.2 us
  Pallas kernels  70.1 us (97%)
  local copies, waits for them, and re-layouts  1.42 us (2%)
    pallas_call x1, Pallas kernels, on_device(): pl.pallas_call(functools.partial(kernel, count, group, subgroups, width,...  70.1 us

profile of v6, /device:TPU:1, one launch (start us, length us, event | category | flops | bytes accessed | tf_op | source)
XLA Modules:
  0.0 72.2 jit_solution(7210656330865363761)
XLA Ops:
  0.6 70.1 %shard_map.68 = (f32[128,256]{1,0:T(8,128)S(1)}, bf16[128,256]{1,0:T(8,128)(2,1)S(1)}) custom-call(bf16[128,8192]{1,0:T(8,128)(2,1)} %bitcast.10, bf16[512,4096]{1,0:T(8,128)(2,1)} %bitcast.8, bf16[512,4096]{1,0:T(8,128)(2,1)} %bitcast.9, s32[64]{0:T(128)} %owner_hbm.1, s32[64,128]{1,0:T(8,128)} %bitcast.11), custom_call_target="tpu_custom_call" | custom-call | tf_op jit(solution)/shard_map/pallas_call | solution.py:403
  70.8 0.8 %copy.7 = f32[2,64,1,256]{3,2,1,0:T(1,128)} copy(f32[2,64,1,256]{3,1,0,2:T(8,128)S(1)} %bitcast.7) | data formatting | bytes 262144
  71.6 0.6 copy.9

commit v7 on v6

--- a/solution.py
+++ b/solution.py
@@ -314,6 +314,13 @@
     multiply(1)
     reduce(2)
     reduce(1)
+    for m in range(3, planes):
+        if m % 2:
+            multiply_staggered(m)
+        else:
+            multiply(m)
+            reduce(m)
+
     def wait_digest(step, carry):
         d_arrival((me + step) % count).wait_recv()
         return carry
@@ -342,17 +349,6 @@
     )
     exchange.start()
 
-    for m in range(3, planes):
-        if m % 2:
-            multiply_staggered(m)
-        else:
-            multiply(m)
-            reduce(m)
-
-    digest_ref[pl.ds(pl.multiple_of(side * blocks, blocks), blocks), :] = dig_mine[...]
-    exchange.wait()
-    digest_ref[pl.ds(pl.multiple_of((1 - side) * blocks, blocks), blocks), :] = dig_theirs[...]
-
     def drain_digest(step, carry):
         d_copy((me + step) % count).wait_send()
         return carry
@@ -370,6 +366,10 @@
 
             lax.fori_loop(1, group + (m > 0), drain_spot, 0)
             lax.fori_loop(1, group, drain_part, 0)
+
+    digest_ref[pl.ds(pl.multiple_of(side * blocks, blocks), blocks), :] = dig_mine[...]
+    exchange.wait()
+    digest_ref[pl.ds(pl.multiple_of((1 - side) * blocks, blocks), blocks), :] = dig_theirs[...]
 
     summed = total[0]
     for m in range(1, planes, 2):

time: 72.3 us -> 64.1 us (0.89)
  Pallas kernels: 70.1 us -> 61.9 us
    pallas_call x1, Pallas kernels: 70.1 us -> 61.9 us  [on_device(): pl.pallas_call(functools.partial(kernel, count, group, subgroups, width,...]
where the time goes in v7:
time: 64.1 us; the launch traced here: 64 us
  Pallas kernels  61.9 us (97%)
  local copies, waits for them, and re-layouts  1.42 us (2%)
    pallas_call x1, Pallas kernels, on_device(): pl.pallas_call(functools.partial(kernel, count, group, subgroups, width,...  61.9 us
    unnamed x2, local copies, waits for them, and re-layouts  1.42 us

profile of v7, /device:TPU:1, one launch (start us, length us, event | category | flops | bytes accessed | tf_op | source)
XLA Modules:
  0.0 64.0 jit_solution(3674419077763478677)
XLA Ops:
  0.6 61.9 %shard_map.68 = (f32[128,256]{1,0:T(8,128)S(1)}, bf16[128,256]{1,0:T(8,128)(2,1)S(1)}) custom-call(bf16[128,8192]{1,0:T(8,128)(2,1)} %bitcast.10, bf16[512,4096]{1,0:T(8,128)(2,1)} %bitcast.8, bf16[512,4096]{1,0:T(8,128)(2,1)} %bitcast.9, s32[64]{0:T(128)} %owner_hbm.1, s32[64,128]{1,0:T(8,128)} %bitcast.11), custom_call_target="tpu_custom_call" | custom-call | tf_op jit(solution)/shard_map/pallas_call | solution.py:403
  62.5 0.8 %copy.7 = f32[2,64,1,256]{3,2,1,0:T(1,128)} copy(f32[2,64,1,256]{3,1,0,2:T(8,128)S(1)} %bitcast.7) | data formatting | bytes 262144
  63.3 0.6 copy.9

commit v8 on v7

--- a/solution.py
+++ b/solution.py
@@ -246,9 +246,10 @@
             if m % 2:
                 send(m + 1, j)
                 return
-            turn = (1 - spot % 2) * 2 if m == 2 else spot % 2
-
-            @pl.when((j - 1) // 2 == turn)
+            if m == 2:
+                return
+
+            @pl.when((j - 1) // 2 == spot % 2)
             def _():
                 send(m + 1, 2 * ((j - 1) % 2) + 1)
                 send(m + 1, 2 * ((j - 1) % 2) + 2)
@@ -275,6 +276,12 @@
                     spot_from = (spot + group - j) % group
                     x_arrival(partner(m) * group + spot_from, half).wait_recv()
                     start_following(m, 2 * odd + step + 1)
+                    if m == 3 and odd == 0:
+                        @pl.when(spot % 2 == 1)
+                        def _():
+                            send(3, 2 * step + 1)
+                            send(3, 2 * step + 2)
+
 
                     @pl.when(j == group)
                     def _():

time: 64.1 us -> 66.3 us (1.034)
  the two profiles are of different devices: /device:TPU:1 before, /device:TPU:9 now
where the time goes in v8:
time: 66.3 us; the launch traced here: 66.2 us
  Pallas kernels  64.1 us (97%)
  local copies, waits for them, and re-layouts  1.42 us (2%)
    pallas_call x1, Pallas kernels, on_device(): pl.pallas_call(functools.partial(kernel, count, group, subgroups, width,...  64.1 us
    unnamed x2, local copies, waits for them, and re-layouts  1.42 us

profile of v8, /device:TPU:9, one launch (start us, length us, event | category | flops | bytes accessed | tf_op | source)
XLA Modules:
  0.0 66.2 jit_solution(13449104944436140764)
XLA Ops:
  0.6 64.1 %shard_map.68 = (f32[128,256]{1,0:T(8,128)S(1)}, bf16[128,256]{1,0:T(8,128)(2,1)S(1)}) custom-call(bf16[128,8192]{1,0:T(8,128)(2,1)} %bitcast.10, bf16[512,4096]{1,0:T(8,128)(2,1)} %bitcast.8, bf16[512,4096]{1,0:T(8,128)(2,1)} %bitcast.9, s32[64]{0:T(128)} %owner_hbm.1, s32[64,128]{1,0:T(8,128)} %bitcast.11), custom_call_target="tpu_custom_call" | custom-call | tf_op jit(solution)/shard_map/pallas_call | solution.py:410
  64.8 0.8 %copy.7 = f32[2,64,1,256]{3,2,1,0:T(1,128)} copy(f32[2,64,1,256]{3,1,0,2:T(8,128)S(1)} %bitcast.7) | data formatting | bytes 262144
  65.6 0.6 copy.9

commit v9 on v8

--- a/solution.py
+++ b/solution.py
@@ -126,9 +126,7 @@
     send_phase(0, group)
     send_phase(1, group + 1)
 
-    @pl.when(spot % 2 == 0)
-    def _():
-        send_phase(3, group + 1)
+    send_phase(3, group + 1)
 
     pick(me, got)
 
@@ -276,12 +274,6 @@
                     spot_from = (spot + group - j) % group
                     x_arrival(partner(m) * group + spot_from, half).wait_recv()
                     start_following(m, 2 * odd + step + 1)
-                    if m == 3 and odd == 0:
-                        @pl.when(spot % 2 == 1)
-                        def _():
-                            send(3, 2 * step + 1)
-                            send(3, 2 * step + 2)
-
 
                     @pl.when(j == group)
                     def _():

time: 66.3 us -> 64.2 us (0.968)
  the two profiles are of different devices: /device:TPU:9 before, /device:TPU:1 now
where the time goes in v9:
time: 64.2 us; the launch traced here: 63.8 us
  Pallas kernels  61.8 us (96%)
  local copies, waits for them, and re-layouts  1.42 us (2%)
    pallas_call x1, Pallas kernels, on_device(): pl.pallas_call(functools.partial(kernel, count, group, subgroups, width,...  61.8 us
    unnamed x2, local copies, waits for them, and re-layouts  1.42 us

profile of v9, /device:TPU:1, one launch (start us, length us, event | category | flops | bytes accessed | tf_op | source)
XLA Modules:
  0.0 63.8 jit_solution(11863319347092567251)
XLA Ops:
  0.6 61.8 %shard_map.68 = (f32[128,256]{1,0:T(8,128)S(1)}, bf16[128,256]{1,0:T(8,128)(2,1)S(1)}) custom-call(bf16[128,8192]{1,0:T(8,128)(2,1)} %bitcast.10, bf16[512,4096]{1,0:T(8,128)(2,1)} %bitcast.8, bf16[512,4096]{1,0:T(8,128)(2,1)} %bitcast.9, s32[64]{0:T(128)} %owner_hbm.1, s32[64,128]{1,0:T(8,128)} %bitcast.11), custom_call_target="tpu_custom_call" | custom-call | tf_op jit(solution)/shard_map/pallas_call | solution.py:402
  62.4 0.8 %copy.7 = f32[2,64,1,256]{3,2,1,0:T(1,128)} copy(f32[2,64,1,256]{3,1,0,2:T(8,128)S(1)} %bitcast.7) | data formatting | bytes 262144
  63.2 0.6 copy.9
